TPU v7x, 512 devices: a whole 4x4x16 slice. The times are simulated.
512 devices in a mesh: blk: 16 (over x, y_lo, core), lane: 32 (over z, y_hi).
Axes of the slice: x: 4, y: 4 (y_hi: 2, y_lo: 2; y = y_hi * 2 + y_lo), z: 16, core: 2. Of those that a mesh axis runs over, the one named last changes fastest.
Arguments:
- positions: float32 [3, 12288], P(None, ('blk', 'lane')), may hold values from -4 to 4
- velocities: float32 [3, 12288], P(None, ('blk', 'lane')), may hold values from -3 to 3
- masses: float32 [12288], P(('blk', 'lane')), may hold values from 0.2 to 5
- tangents: float32 [6, 12288, 128], P(None, ('blk', 'lane')), may hold values from -14 to 14
Outputs:
- new_positions: float32 [3, 12288], P(None, ('blk', 'lane'))
- new_velocities: float32 [3, 12288], P(None, ('blk', 'lane'))
- basis: float32 [6, 12288, 128], P(None, ('blk', 'lane'))
- growth: float32 [128, 128], replicated
All inputs are finite; a program needn't handle non-finite values.
Results may differ from a plain program's by a relative error of at most 0.0003.
Values sent between devices are 32-bit elements; how exact they have to be, the bound alone decides.
A program may use at most 64 MiB of HBM per device.

v0:
```python
import jax
import jax.numpy as jnp
from jax import lax
from jax.sharding import PartitionSpec as P

STEP = 0.0625
SOFT = 0.0025


def body(positions, velocities, masses, tangents):
    half_step = 0.5 * STEP
    own_count = positions.shape[1]
    vectors = tangents.shape[2]
    total_stars = own_count * lax.axis_size("blk") * lax.axis_size("lane")
    mass_row = (masses / total_stars)[None, :]
    pos_half = positions + half_step * velocities
    dx_half = tangents[:3] + half_step * tangents[3:]
    targets = lax.all_gather(pos_half, "lane", axis=1, tiled=True)
    target_count = targets.shape[1]
    identity = jnp.eye(3, dtype=jnp.float32)
    source_pos = lax.all_gather(pos_half, "blk", axis=1, tiled=True)
    source_mass = lax.all_gather(mass_row, "blk", axis=1, tiled=True)
    source_dx = lax.all_gather(dx_half, "blk", axis=1, tiled=True)
    offsets = source_pos[:, None, :] - targets[:, :, None]
    squared = jnp.sum(offsets * offsets, axis=0) + SOFT
    inverse = lax.rsqrt(squared)
    near_weight = source_mass * inverse * inverse * inverse
    tide_weight = near_weight / squared
    accel_sum = jnp.sum(near_weight[None] * offsets, axis=2)
    kernel = (
        identity[:, None, :, None] * near_weight[None, :, None, :]
        - 3.0
        * tide_weight[None, :, None, :]
        * offsets[:, :, None, :]
        * jnp.transpose(offsets, (1, 0, 2))[None]
    )
    row_total = jnp.transpose(jnp.sum(kernel, axis=3), (0, 2, 1)).reshape(9, target_count)
    stacked = source_dx.reshape(-1, vectors)
    pull_total = jnp.einsum(
        "aij,jk->aik",
        kernel.reshape(3, target_count, -1),
        stacked,
        precision=lax.Precision.HIGHEST,
        preferred_element_type=jnp.float32,
    )
    summed = lax.psum((accel_sum, row_total, pull_total), "lane")
    offset = lax.axis_index("lane") * own_count
    acceleration = lax.dynamic_slice_in_dim(summed[0], offset, own_count, 1)
    row_sums = lax.dynamic_slice_in_dim(summed[1], offset, own_count, 1)
    tangent_pull = lax.dynamic_slice_in_dim(summed[2], offset, own_count, 1)
    tangent_pull = tangent_pull - jnp.sum(
        row_sums.reshape(3, 3, own_count)[:, :, :, None] * dx_half[None], axis=1
    )
    new_velocities = velocities + STEP * acceleration
    dv_new = tangents[3:] + STEP * tangent_pull
    new_positions = pos_half + half_step * new_velocities
    dx_new = dx_half + half_step * dv_new
    matrix = jnp.concatenate([dx_new, dv_new], axis=0).reshape(-1, vectors)
    local_gram = jnp.dot(
        matrix.T, matrix, precision=lax.Precision.HIGHEST, preferred_element_type=jnp.float32
    )
    gram = lax.psum(local_gram, ("blk", "lane")) / jnp.float32(6 * total_stars)
    lower = jnp.linalg.cholesky(gram)
    growth = lower.T
    basis = jax.scipy.linalg.solve_triangular(lower, matrix.T, lower=True).T.reshape(
        6, own_count, vectors
    )
    return (new_positions, new_velocities, basis, growth)


def solution(mesh):
    return jax.shard_map(
        body,
        mesh=mesh,
        in_specs=(
            P(None, ("blk", "lane")),
            P(None, ("blk", "lane")),
            P(("blk", "lane")),
            P(None, ("blk", "lane"), None),
        ),
        out_specs=(
            P(None, ("blk", "lane")),
            P(None, ("blk", "lane")),
            P(None, ("blk", "lane"), None),
            P(),
        ),
        check_vma=False,
    )
```

profile of v0, /device:TPU:1, one launch (start us, length us, event | category | flops | bytes accessed | tf_op | source)
XLA Modules:
  0.0 959.0 jit_solution(11230009136783589848)
XLA Ops:
  7.9 69.5 %all-gather.2 = f32[32,24,3]{1,2,0:T(4,128)S(1)} all-gather(f32[1,24,3]{1,2,0:T(4,128)S(1)} %fusion.15), channel_id=1, replica_groups=mesh['blk'=16,'lane'=32] {'lane'}, dimensions={0}, use_global_device_ids=true | all-gather | bytes 9504 | tf_op jit(solution)/shard_map/all_gather | solution.py:18
  77.4 33.5 %all-gather.1 = f32[16,24,3]{1,2,0:T(4,128)S(1)} all-gather(f32[1,24,3]{1,2,0:T(4,128)S(1)} %fusion.15), channel_id=1, replica_groups=mesh['blk'=16,'lane'=32] {'blk'}, dimensions={0}, use_global_device_ids=true | all-gather | bytes 4896 | tf_op jit(solution)/shard_map/all_gather | solution.py:21
  111.7 1.1 broadcast_subtract_fusion
  112.9 1.4 fusion.6
  114.3 1.3 dynamic-slice
  116.8 1.3 multiply_dynamic-update-slice_fusion
  118.1 27.3 %all-reduce = f32[384]{0:T(512)} all-reduce(f32[384]{0:T(512)} %multiply_dynamic-update-slice_fusion), channel_id=2, replica_groups=mesh['blk'=16,'lane'=32] {'blk'}, use_global_device_ids=true, to_apply=%add | all-reduce | flops 384 | bytes 3072
  146.9 18.6 %all_gather.18 = f32[3,384,128]{2,1,0:T(8,128)S(1)} all-gather(f32[3,24,128]{2,1,0:T(8,128)S(1)} %multiply_add_fusion.2), channel_id=1, replica_groups=mesh['blk'=16,'lane'=32] {'blk'}, dimensions={1}, use_global_device_ids=true | all-gather | bytes 626688 | tf_op jit(solution)/shard_map/all_gather | solution.py:23
  165.5 1.7 divide_multiply_fusion
  167.2 1.6 subtract_multiply_fusion
  168.8 1.8 copy-done
  170.5 10.5 %fusion.8 = f32[3,768,128]{2,1,0:T(8,128)} fusion(f32[768,3,384]{2,0,1:T(8,128)S(1)} %broadcast_subtract_fusion, f32[3,768,384]{2,1,0:T(8,128)S(1)} %get-tuple-element.30, f32[768,384]{1,0:T(8,128)S(1)} %get-tuple-element.27, f32[3,3]{1,0:T(4,128)S(1)} %fusion.14, f32[3,384,128]{2,1,0:T(8,128)S(1)} %all_gather.18), kind=kOutput, calls=%fused_computation.14 | convolution fusion | flops 4084826112 | bytes 10027044 | tf_op jit(solution)/shard_map/aij,jk->aik/dot_general | solution.py:39
  181.3 4.5 fusion
  186.6 118.4 %all-reduce.1 = (f32[3,768]{1,0:T(4,128)S(1)}, f32[9,768]{1,0:T(8,128)S(1)}) all-reduce(f32[3,768]{1,0:T(4,128)S(1)} %copy-done.5, f32[9,768]{1,0:T(8,128)S(1)} %reshape.112), channel_id=1, replica_groups=mesh['blk'=16,'lane'=32] {'lane'}, use_global_device_ids=true, to_apply=%region_2.0 | all-reduce | flops 9216 | bytes 73728 | tf_op jit(solution)/shard_map/psum | solution.py:46
  305.1 0.9 multiply_reduce_fusion
  306.0 156.5 %all-reduce.5.cloned.1.call-done = f32[3,768,128]{2,1,0:T(8,128)} async-done(((f32[3,768,128]{2,1,0:T(8,128)}), f32[3,768,128]{2,1,0:T(8,128)}) %all-reduce.5.cloned.1.call-update) | async-done | bytes 1179664 | tf_op jit(solution)/shard_map/psum | solution.py:46
  463.3 1.1 convolution_bitcast_fusion
  464.4 1.4 multiply_add_fusion.3
  465.8 460.1 %all-reduce.7.cloned.1.call-done = f32[128,128]{0,1:T(8,128)} async-done(((f32[128,128]{0,1:T(8,128)}), f32[128,128]{0,1:T(8,128)}) %all-reduce.7.cloned.1.call-update) | async-done | bytes 65552 | tf_op jit(solution)/shard_map/psum | solution.py:62
  925.9 0.8 broadcast_multiply_fusion
  926.9 0.9 fusion.12
  927.7 11.7 %cholesky.16 = f32[128,128]{1,0:T(8,128)S(1)} custom-call(f32[128,128]{1,0:T(8,128)S(1)} %fusion.12), custom_call_target="Cholesky" | custom-call | tf_op jit(solution)/shard_map/jit(cholesky)/cholesky | solution.py:63
  940.8 9.8 %custom-call.7 = f32[1,128,128]{1,2,0:T(8,128)S(1)} custom-call(f32[1,128,128]{2,1,0:T(8,128)S(1)} %get-tuple-element.29), custom_call_target="InvertDiagBlocksLowerTriangular" | custom-call | tf_op jit(solution)/shard_map/jit(_solve_triangular)/triangular_solve | solution.py:65
  950.6 0.8 fusion.10
  (32 shorter events, 7.6 us)
Async XLA Ops:
  7.2 455.3 %all-reduce.5.cloned.1.call-start = ((), (), s32[]{:S(2)}) async-start(), calls=%async_computation | async-start | bytes 2359296 | tf_op jit(solution)/shard_map/psum | solution.py:46
  111.7 1.1 copy-start.3
  145.5 21.7 %copy-start.4 = (f32[384,3]{0,1:T(4,128)S(1)}, f32[384,3]{0,1:T(4,128)}, u32[]{:S(2)}) copy-start(f32[384,3]{0,1:T(4,128)} %reshape.119) | copy-start | bytes 13828
  146.3 0.6 copy-start.2
  167.2 1.6 copy-start.1
  168.8 1.8 copy-start
  181.1 5.5 copy-start.5
  181.1 744.8 %all-reduce.7.cloned.1.call-start = ((), (), s32[]{:S(2)}) async-start(), calls=%async_computation.1 | async-start | bytes 131072 | tf_op jit(solution)/shard_map/psum | solution.py:62
Sparse Core Ops, SparseCore 0:
  181.2 281.2 all-reduce.4
  469.4 456.4 all-reduce.6
where the time goes:
time: 960 us; the launch traced here: 959 us
  waiting for transfers between devices  617 us (64%)
  blocking collectives  267 us (28%)
  other arithmetic  40.7 us (4%)
  between operations  14.8 us (2%)
  matrix products  12.4 us (1%)
    psum x1, waiting for transfers between devices, body(): gram = lax.psum(local_gram, ('blk', 'lane')) / jnp.float32(6 * total_stars)  460 us
    psum x1, waiting for transfers between devices, body(): summed = lax.psum((accel_sum, row_total, pull_total), 'lane')  157 us
    psum x1, blocking collectives, body(): summed = lax.psum((accel_sum, row_total, pull_total), 'lane')  118 us
    all_gather x1, blocking collectives, body(): targets = lax.all_gather(pos_half, 'lane', axis=1, tiled=True)  69.5 us
    all_gather x1, blocking collectives, body(): source_pos = lax.all_gather(pos_half, 'blk', axis=1, tiled=True)  33.5 us
    unnamed x1, blocking collectives  27.3 us
  transfers between devices with their start and end apart: 2, of which 2 were waited for; matrix products, arithmetic and copies ran while one was open for 1% of the time, Pallas kernels for 0%

commit v1 on v0

v1 whole, which is shorter than its diff:
```python
import functools

import jax
import jax.numpy as jnp
from jax import lax
from jax.experimental import pallas as pl
from jax.experimental.pallas import tpu as pltpu
from jax.sharding import PartitionSpec as P

STEP = 0.0625
SOFT = 0.0025
HALF = 0.5 * STEP
MESH = pl.DeviceIdType.MESH
HIGHEST = lax.Precision.HIGHEST
Y = 4


def lane_iota(shape):
    return lax.broadcasted_iota(jnp.int32, shape, 1)


def pack_lanes(tiles, width):
    pieces = [None] * ((len(tiles) * width + 127) // 128)
    lanes = lane_iota((8, 128))

    def put(index, value):
        pieces[index] = value if pieces[index] is None else pieces[index] + value

    for index, tile in enumerate(tiles):
        chunk, offset = divmod(index * width, 128)
        turned = pltpu.roll(tile, offset, 1) if offset else tile
        if offset + width > 128:
            put(chunk, jnp.where(lanes >= offset, turned, 0.0))
            put(chunk + 1, jnp.where(lanes < offset, turned, 0.0))
        else:
            put(chunk, turned)
    return pieces


def step_kernel(
    xs, zs, n, total,
    pos_ref, vel_ref, mass_ref, tan_ref,
    gram_ref, mat_ref, npos_ref, nvel_ref,
    row_z, row_p, dx_buf, src, tgt, k_hi, k_lo, dx_b,
    ext_send, ext_recv, out_send, out_recv,
    g_own, g_sib, g_half, g_plane, g_mine, g_line, g_all,
    pz_send, pz_recv, pp_send, pp_recv, ps_send, ps_recv,
    up_send, up_recv, dn_send, dn_recv, sh_send, sh_recv,
    ex_send, ex_recv, rs_send, rs_recv, gs_send, gs_recv,
):
    blk, lane = lax.axis_index("blk"), lax.axis_index("lane")
    core = lax.rem(blk, 2)
    px = blk // 4
    py = lax.rem(lane, 2) * 2 + lax.rem(blk // 2, 2)
    z = lane // 2
    planes = xs * Y
    targets = planes * n
    sources = 2 * zs * n
    up_steps, dn_steps = zs // 2, (zs - 1) // 2

    def plane_peer(i, j):
        ox, oy = lax.rem(px + i, xs), lax.rem(py + j, Y)
        return (ox * 4 + lax.rem(oy, 2) * 2 + core, z * 2 + oy // 2), ox * Y + oy

    def plane_back(i, j):
        return lax.rem(xs - i, xs) * Y + lax.rem(Y - j, Y)

    def line_peer(r):
        return (blk, lax.rem(z + r, zs) * 2 + lax.rem(lane, 2))

    sibling = (blk + 1 - 2 * core, lane)
    here = px * Y + py

    def remote(source, target, send_sem, recv_sem, device):
        return pltpu.make_async_remote_copy(
            src_ref=source, dst_ref=target, send_sem=send_sem, recv_sem=recv_sem,
            device_id=device, device_id_type=MESH,
        )

    barrier = pltpu.get_barrier_semaphore()
    for r in range(1, zs):
        pl.semaphore_signal(barrier, inc=1, device_id=line_peer(r), device_id_type=MESH)
    for t in range(1, planes):
        pl.semaphore_signal(barrier, inc=1, device_id=plane_peer(t // Y, t % Y)[0], device_id_type=MESH)
    pl.semaphore_signal(barrier, inc=1, device_id=sibling, device_id_type=MESH)

    pos_half = pos_ref[...] + HALF * vel_ref[...]
    row_z[0, 0] = jnp.zeros((8, 128), jnp.float32)
    row_z[0, 0, 0:3, 0:n] = pos_half
    row_z[0, 0, 3:4, 0:n] = mass_ref[...] / total
    row_p[0] = row_z[0, 0]
    dx_half = tan_ref[0:3] + HALF * tan_ref[3:6]
    dx_buf[:, 0, 0] = dx_half
    pl.semaphore_wait(barrier, zs - 1 + planes - 1 + 1)

    for r in range(1, zs):
        remote(row_z.at[0, 0], row_z.at[0, zs - r], pz_send, pz_recv, line_peer(r)).start()
    for t in range(1, planes):
        remote(row_z.at[0, 0], row_p.at[plane_back(t // Y, t % Y)], pp_send, pp_recv, plane_peer(t // Y, t % Y)[0]).start()

    def up_copy(s):
        return remote(
            dx_buf.at[:, 0, (zs - s + 1) % zs], dx_buf.at[:, 0, zs - s],
            up_send.at[s - 1], up_recv.at[s - 1], line_peer(1),
        )

    def dn_copy(s):
        return remote(
            dx_buf.at[:, 0, s - 1], dx_buf.at[:, 0, s],
            dn_send.at[s - 1], dn_recv.at[s - 1], line_peer(zs - 1),
        )

    def share(r):
        return remote(dx_buf.at[:, 0, r], dx_buf.at[:, 1, r], sh_send.at[r], sh_recv.at[r], sibling)

    def advance(s):
        up_copy(s).wait_recv()
        if s + 1 <= up_steps:
            up_copy(s + 1).start()
        if s <= dn_steps:
            dn_copy(s).wait_recv()
            if s + 1 <= dn_steps:
                dn_copy(s + 1).start()
        share(zs - s).start()
        if s <= dn_steps:
            share(s).start()

    up_copy(1).start()
    if dn_steps:
        dn_copy(1).start()
    share(0).start()

    remote(row_z.at[0, pl.ds(1, zs - 1)], row_z.at[0, pl.ds(1, zs - 1)], pz_send, pz_recv, sibling).wait_recv()
    line_share = remote(row_z.at[0], row_z.at[1], ps_send, ps_recv, sibling)
    line_share.start()
    remote(row_p.at[pl.ds(1, planes - 1)], row_p.at[pl.ds(1, planes - 1)], pp_send, pp_recv, sibling).wait_recv()
    for c, piece in enumerate(pack_lanes([row_p[t] for t in range(planes)], n)):
        tgt[c * 128:(c + 1) * 128, 0:8] = piece.T
    advance(1)
    line_share.wait_recv()
    tiles = [row_z[h, r] for h in range(2) for r in range(zs)]
    for c, piece in enumerate(pack_lanes(tiles, n)):
        src[:, c * 128:(c + 1) * 128] = piece

    subs = 2 * n // 16
    lanes16 = lane_iota((16, 128))

    def pair_block(b, _):
        pair, sub = b // subs, lax.rem(b, subs)
        base = pair * (6 * n) + sub * 16
        place = tgt[pl.ds(pl.multiple_of(b * 16, 16), 16), 0:8]
        own = [jnp.broadcast_to(place[:, a:a + 1], (16, 128)) for a in range(3)]
        sums = [None] * 9
        for c in range(sources // 128):
            columns = pl.ds(c * 128, 128)
            d = [src[a:a + 1, columns] - own[a] for a in range(3)]
            squared = d[0] * d[0] + d[1] * d[1] + d[2] * d[2] + SOFT
            inverse = lax.rsqrt(squared)
            inverse2 = inverse * inverse
            near = src[3:4, columns] * inverse * inverse2
            tide = 3.0 * near * inverse2
            td = [tide * d[a] for a in range(3)]
            part = {}
            for a in range(3):
                for e in range(a, 3):
                    product = td[a] * d[e]
                    part[a, e] = near - product if a == e else -product
            terms = [near * d[a] for a in range(3)] + [part[a, e] for a in range(3) for e in range(a, 3)]
            sums = [t if s is None else s + t for s, t in zip(sums, terms)]
            for a in range(3):
                for e in range(a, 3):
                    high = part[a, e].astype(jnp.bfloat16)
                    low = (part[a, e] - high.astype(jnp.float32)).astype(jnp.bfloat16)
                    for f, g in {(a, e), (e, a)}:
                        where = (pl.ds(pl.multiple_of(base + f * 2 * n, 16), 16), pl.ds(g * sources + c * 128, 128))
                        k_hi[where] = high
                        k_lo[where] = low
        tile = jnp.zeros((16, 128), jnp.float32)
        for k, s in enumerate(sums):
            tile = jnp.where(lanes16 == k, jnp.sum(s, axis=1, keepdims=True), tile)
        ext_send[pl.ds(pl.multiple_of(b * 16, 16), 16), :] = tile
        return 0

    blocks = targets // 16
    slots = max(up_steps - 1, 1)
    done = 0
    for s in range(2, up_steps + 1):
        upto = blocks * (s - 1) // slots
        lax.fori_loop(done, upto, pair_block, 0)
        done = upto
        advance(s)

    for t in range(1, planes):
        back = plane_back(t // Y, t % Y)
        remote(
            ext_send.at[pl.ds(t * n, n)], ext_recv.at[back - 1], ex_send, ex_recv, plane_peer(t // Y, t % Y)[0]
        ).start()

    for r in range(zs):
        share(r).wait_recv()
    for b in range(3):
        for h in range(2):
            block = dx_buf[b, h].reshape(zs * n, 128)
            high = block.astype(jnp.bfloat16)
            low = (block - high.astype(jnp.float32)).astype(jnp.bfloat16)
            start = b * sources + h * zs * n
            dx_b[start:start + zs * n, 0:128] = high
            dx_b[start:start + zs * n, 128:256] = low

    group = 4
    rows = group * 3 * n

    def pull_group(g, _):
        where = pl.ds(pl.multiple_of(g * rows, 16), rows)
        first = jnp.dot(k_hi[where, :], dx_b[...], preferred_element_type=jnp.float32)
        second = jnp.dot(k_lo[where, :], dx_b[:, 0:128], preferred_element_type=jnp.float32)
        pulled = first[:, 0:128] + (first[:, 128:256] + second)
        out_send[pl.ds(g * (group // 2), group // 2)] = pulled.reshape(group // 2, 3, 2, n, 128)
        for u in range(group):
            t = g * group + u
            i, j = t // Y, lax.rem(t, Y)

            @pl.when(t != 0)
            def _():
                remote(
                    out_send.at[t // 2, :, lax.rem(t, 2)], out_recv.at[plane_back(i, j) - 1],
                    rs_send, rs_recv, plane_peer(i, j)[0],
                ).start()

        return 0

    lax.fori_loop(0, planes // group, pull_group, 0)

    remote(ext_recv, ext_recv, ex_send, ex_recv, sibling).wait_recv()
    extra = ext_send[0:n, :]
    for t in range(planes - 1):
        extra = extra + ext_recv[t]
    acceleration = extra.T[0:3, :]
    new_velocities = vel_ref[...] + STEP * acceleration
    nvel_ref[...] = new_velocities
    npos_ref[...] = pos_half + HALF * new_velocities
    index = {}
    for a in range(3):
        for e in range(a, 3):
            index[a, e] = index[e, a] = 3 + len(set(index.values()))
    offset = []
    for a in range(3):
        taken = 0.0
        for e in range(3):
            taken = taken + extra[:, index[a, e]:index[a, e] + 1] * dx_buf[e, 0, 0]
        offset.append(taken)

    remote(out_recv, out_recv, rs_send, rs_recv, sibling).wait_recv()
    for a in range(3):
        pulled = out_send[0, a, 0]
        for t in range(planes - 1):
            pulled = pulled + out_recv[t, a]
        dv_new = tan_ref[3 + a] + STEP * (pulled - offset[a])
        mat_ref[3 + a] = dv_new
        mat_ref[a] = dx_buf[a, 0, 0] + HALF * dv_new
    matrix = mat_ref[...].reshape(6 * n, 128)
    gram = lax.dot_general(
        matrix, matrix, (((0,), (0,)), ((), ())), precision=HIGHEST, preferred_element_type=jnp.float32
    )

    part_rows = 64 // planes
    g_own[...] = gram.reshape(2, planes, part_rows, 128)
    first = remote(g_own.at[1 - core], g_sib, gs_send.at[0], gs_recv.at[0], sibling)
    first.start()
    first.wait_recv()
    g_half[...] = g_own[core] + g_sib[...]
    for t in range(1, planes):
        device, place = plane_peer(t // Y, t % Y)
        remote(
            g_half.at[place], g_plane.at[plane_back(t // Y, t % Y) - 1], gs_send.at[1], gs_recv.at[1], device
        ).start()
    remote(g_plane, g_plane, gs_send.at[1], gs_recv.at[1], sibling).wait_recv()
    mine = g_half[here]
    for t in range(planes - 1):
        mine = mine + g_plane[t]
    g_mine[...] = mine
    for r in range(1, zs):
        remote(g_mine, g_line.at[zs - r - 1], gs_send.at[2], gs_recv.at[2], line_peer(r)).start()
    remote(g_line, g_line, gs_send.at[2], gs_recv.at[2], sibling).wait_recv()
    for r in range(zs - 1):
        mine = mine + g_line[r]
    g_all[core, here] = mine / (6.0 * total)
    for t in range(1, planes):
        remote(
            g_all.at[core, here], g_all.at[core, here], gs_send.at[3], gs_recv.at[3], plane_peer(t // Y, t % Y)[0]
        ).start()
    some = g_all.at[core, pl.ds(0, planes - 1)]
    remote(some, some, gs_send.at[3], gs_recv.at[3], sibling).wait_recv()
    last = remote(g_all.at[core], g_all.at[core], gs_send.at[4], gs_recv.at[4], sibling)
    last.start()
    last.wait_recv()
    gram_ref[...] = g_all[...].reshape(128, 128)

    remote(row_z.at[0, pl.ds(1, zs - 1)], row_z.at[0, pl.ds(1, zs - 1)], pz_send, pz_recv, sibling).wait_send()
    remote(row_p.at[pl.ds(1, planes - 1)], row_p.at[pl.ds(1, planes - 1)], pp_send, pp_recv, sibling).wait_send()
    line_share.wait_send()
    for s in range(1, up_steps + 1):
        up_copy(s).wait_send()
        if s <= dn_steps:
            dn_copy(s).wait_send()
    for r in range(zs):
        share(r).wait_send()
    remote(ext_recv, ext_recv, ex_send, ex_recv, sibling).wait_send()
    remote(out_recv, out_recv, rs_send, rs_recv, sibling).wait_send()
    first.wait_send()
    remote(g_plane, g_plane, gs_send.at[1], gs_recv.at[1], sibling).wait_send()
    remote(g_line, g_line, gs_send.at[2], gs_recv.at[2], sibling).wait_send()
    remote(some, some, gs_send.at[3], gs_recv.at[3], sibling).wait_send()
    last.wait_send()


def factor_kernel(gram_ref, mat_ref, npos_ref, nvel_ref, pos_out, vel_out, basis_out, growth_out):
    k = gram_ref.shape[0]
    count = k // 8
    pos_out[...] = npos_ref[...]
    vel_out[...] = nvel_ref[...]
    lanes = lane_iota((8, k))
    rows = lax.broadcasted_iota(jnp.int32, (8, k), 0)
    a = [gram_ref[8 * i:8 * i + 8, :] for i in range(count)]
    q = [jnp.where(lanes == rows + 8 * i, 1.0, 0.0) for i in range(count)]
    full = lambda row: jnp.broadcast_to(row, (8, k))
    inverse_rows = []
    for b in range(count):
        c = {
            i: [jnp.broadcast_to(a[i][:, 8 * b + e:8 * b + e + 1], (8, k)) for e in range(8)]
            for i in range(b, count)
        }
        scale = jnp.ones((8, k), jnp.float32)
        for r in range(8):
            arow, qrow = full(a[b][r:r + 1, :]), full(q[b][r:r + 1, :])
            crow = {e: full(c[b][e][r:r + 1, :]) for e in range(r, 8)}
            scale = jnp.where(rows == r, lax.rsqrt(crow[r]), scale)
            inverse = 1.0 / crow[r]
            for i in range(b, count):
                m = c[i][r] * inverse
                if i == b:
                    m = jnp.where(rows > r, m, 0.0)
                a[i] = a[i] - m * arow
                q[i] = q[i] - m * qrow
                for e in range(r + 1, 8):
                    c[i][e] = c[i][e] - m * crow[e]
        growth_out[8 * b:8 * b + 8, :] = jnp.where(lanes >= rows + 8 * b, a[b] * scale, 0.0)
        inverse_rows.append(q[b] * scale)
    inverse = jnp.concatenate(inverse_rows, axis=0)
    matrix = mat_ref[...].reshape(-1, k)
    basis = lax.dot_general(
        matrix, inverse, (((1,), (1,)), ((), ())), precision=HIGHEST, preferred_element_type=jnp.float32
    )
    basis_out[...] = basis.reshape(basis_out.shape)


def body(positions, velocities, masses, tangents):
    n, k = positions.shape[1], tangents.shape[2]
    xs, zs = lax.axis_size("blk") // 4, lax.axis_size("lane") // 2
    planes = xs * Y
    total = float(n * planes * zs * 2)
    targets, sources = planes * n, 2 * zs * n
    f32, bf16 = jnp.float32, jnp.bfloat16
    vmem = pl.BlockSpec(memory_space=pltpu.VMEM)
    dma = pltpu.SemaphoreType.DMA
    part_rows = 64 // planes
    scratch = [
        pltpu.VMEM((2, zs, 8, 128), f32),
        pltpu.VMEM((planes, 8, 128), f32),
        pltpu.VMEM((3, 2, zs, n, k), f32),
        pltpu.VMEM((8, sources), f32),
        pltpu.VMEM(((targets + 127) // 128 * 128, 128), f32),
        pltpu.VMEM((3 * targets, 3 * sources), bf16),
        pltpu.VMEM((3 * targets, 3 * sources), bf16),
        pltpu.VMEM((3 * sources, 2 * k), bf16),
        pltpu.VMEM((targets, 128), f32),
        pltpu.VMEM((planes - 1, n, 128), f32),
        pltpu.VMEM((planes // 2, 3, 2, n, k), f32),
        pltpu.VMEM((planes - 1, 3, n, k), f32),
        pltpu.VMEM((2, planes, part_rows, k), f32),
        pltpu.VMEM((planes, part_rows, k), f32),
        pltpu.VMEM((planes, part_rows, k), f32),
        pltpu.VMEM((planes - 1, part_rows, k), f32),
        pltpu.VMEM((part_rows, k), f32),
        pltpu.VMEM((zs - 1, part_rows, k), f32),
        pltpu.VMEM((2, planes, part_rows, k), f32),
        dma, dma, dma, dma, dma, dma,
        dma((zs // 2,)), dma((zs // 2,)), dma((zs // 2,)), dma((zs // 2,)),
        dma((zs,)), dma((zs,)),
        dma, dma, dma, dma, dma((5,)), dma((5,)),
    ]
    gram, matrix, npos, nvel = pl.pallas_call(
        functools.partial(step_kernel, xs, zs, n, total),
        out_shape=[
            jax.ShapeDtypeStruct((k, k), f32),
            jax.ShapeDtypeStruct((6, n, k), f32),
            jax.ShapeDtypeStruct((3, n), f32),
            jax.ShapeDtypeStruct((3, n), f32),
        ],
        in_specs=[vmem] * 4,
        out_specs=[vmem] * 4,
        scratch_shapes=scratch,
        compiler_params=pltpu.CompilerParams(
            collective_id=0, has_side_effects=True, vmem_limit_bytes=40 * 1024 * 1024
        ),
    )(positions, velocities, masses.reshape(1, n), tangents)
    npos, nvel, basis, growth = pl.pallas_call(
        factor_kernel,
        out_shape=[
            jax.ShapeDtypeStruct((3, n), f32),
            jax.ShapeDtypeStruct((3, n), f32),
            jax.ShapeDtypeStruct((6, n, k), f32),
            jax.ShapeDtypeStruct((k, k), f32),
        ],
        in_specs=[vmem] * 4,
        out_specs=[vmem] * 4,
        compiler_params=pltpu.CompilerParams(vmem_limit_bytes=40 * 1024 * 1024),
    )(gram, matrix, npos, nvel)
    return (npos, nvel, basis, growth)


def solution(mesh):
    return jax.shard_map(
        body,
        mesh=mesh,
        in_specs=(
            P(None, ("blk", "lane")),
            P(None, ("blk", "lane")),
            P(("blk", "lane")),
            P(None, ("blk", "lane"), None),
        ),
        out_specs=(
            P(None, ("blk", "lane")),
            P(None, ("blk", "lane")),
            P(None, ("blk", "lane"), None),
            P(),
        ),
        check_vma=False,
    )
```

time: 960 us -> 88.9 us (0.09)
  waiting for transfers between devices: 617 us -> 0 us
  blocking collectives: 267 us -> 0 us
  Pallas kernels: 0 us -> 85.1 us
  other arithmetic: 40.7 us -> 0 us
  between operations: 14.8 us -> 0.65 us
  matrix products: 12.4 us -> 0 us
    psum x2 -> x0, waiting for transfers between devices: 617 us -> none  [the longest x1 460 us: body(): gram = lax.psum(local_gram, ('blk', 'lane')) / jnp.float32(6 * total_stars)]
    all_gather x3 -> x0, blocking collectives: 122 us -> none  [the longest x1 69.5 us: body(): targets = lax.all_gather(pos_half, 'lane', axis=1, tiled=True)]
    psum x1 -> x0, blocking collectives: 118 us -> none  [body(): summed = lax.psum((accel_sum, row_total, pull_total), 'lane')]
    pallas_call x0 -> x2, Pallas kernels: none -> 85.1 us  [the longest x1 80.2 us: body(): pl.pallas_call(functools.partial(step_kernel, xs, zs, n, total), out_shap...]
    unnamed x1 -> x0, blocking collectives: 27.3 us -> none
    another operation x4 -> x0, other arithmetic: 22.2 us -> none  [the longest x3 12.4 us: body(): lower = jnp.linalg.cholesky(gram)]
    dot_general x2 -> x0, matrix products: 11.6 us -> none  [the longest x1 10.5 us: body(): jnp.einsum('aij,jk->aik', kernel.reshape(3, target_count, -1), stacked, p...]
  transfers between devices with their start and end apart: 2 -> 0, of which waited for: 2 -> 0; matrix products, arithmetic and copies ran while one was open for 1% -> 0% of each run, Pallas kernels for 0% -> 0%
where the time goes in v1:
time: 88.9 us; the launch traced here: 88.6 us
  Pallas kernels  85.1 us (96%)
  local copies, waits for them, and re-layouts  2.89 us (3%)
    pallas_call x1, Pallas kernels, body(): pl.pallas_call(functools.partial(step_kernel, xs, zs, n, total), out_shap...  80.2 us
    pallas_call x1, Pallas kernels, body(): pl.pallas_call(factor_kernel, out_shape=[jax.ShapeDtypeStruct((3, n), f32...  4.92 us
    unnamed x8, local copies, waits for them, and re-layouts  2.89 us

profile of v1, /device:TPU:1, one launch (start us, length us, event | category | flops | bytes accessed | tf_op | source)
XLA Modules:
  0.0 88.6 jit_solution(16033670168734837020)
XLA Ops:
  0.6 0.0 copy-start.3
  0.6 0.6 copy-done.3
  1.3 0.0 copy-start
  1.3 0.9 copy-done
  2.2 0.0 copy-start.1
  2.2 0.7 copy-done.1
  2.9 0.0 copy-start.2
  2.9 0.7 copy-done.2
  3.5 80.2 %shard_map.75 = (f32[128,128]{1,0:T(8,128)S(1)}, f32[6,24,128]{2,1,0:T(8,128)S(1)}, f32[3,24]{1,0:T(4,128)S(1)}, f32[3,24]{1,0:T(4,128)S(1)}) custom-call(f32[3,24]{1,0:T(4,128)S(1)} %copy-done.1, f32[3,24]{1,0:T(4,128)S(1)} %copy-done.2, f32[1,24]{1,0:T(1,128)S(1)} %bitcast.1, f32[6,24,128]{2,1,0:T(8,128)S(1)} %copy-done), custom_call_target="tpu_custom_call" | custom-call | tf_op jit(solution)/shard_map/pallas_call | solution.py:392
  83.7 4.9 %shard_map.76 = (f32[3,24]{1,0:T(4,128)}, f32[3,24]{1,0:T(4,128)}, f32[6,24,128]{2,1,0:T(8,128)}, f32[128,128]{1,0:T(8,128)}) custom-call(f32[128,128]{1,0:T(8,128)S(1)} %get-tuple-element.8.gram_ref, f32[6,24,128]{2,1,0:T(8,128)S(1)} %get-tuple-element.9.mat_ref, f32[3,24]{1,0:T(4,128)S(1)} %get-tuple-element.10.npos_ref, ...), custom_call_target="tpu_custom_call" | custom-call | tf_op jit(solution)/shard_map/pallas_call | solution.py:407
Async XLA Ops:
  0.6 0.7 copy-start.3
  1.3 0.9 copy-start
  2.2 0.7 copy-start.1
  2.9 0.7 copy-start.2

commit v2 on v1

--- a/solution.py
+++ b/solution.py
@@ -15,13 +15,22 @@
 Y = 4
 
 
+RING = {
+    16: (
+        {0: (3, -3, 1, -1), 3: (6, 2, 4), -3: (-6, -2, -4), 6: (8, 5, 7), -6: (-5, -7)},
+        ((3, -3, 1, -1), (6, -6, 2, -2, 4, -4), (5, -5, 7, -7, 8)),
+    ),
+    4: ({0: (1, -1), 1: (2,)}, ((1,), (-1,), (2,))),
+}
+
+
 def lane_iota(shape):
     return lax.broadcasted_iota(jnp.int32, shape, 1)
 
 
 def pack_lanes(tiles, width):
     pieces = [None] * ((len(tiles) * width + 127) // 128)
-    lanes = lane_iota((8, 128))
+    lanes = lane_iota((4, 128))
 
     def put(index, value):
         pieces[index] = value if pieces[index] is None else pieces[index] + value
@@ -39,13 +48,14 @@
 
 def step_kernel(
     xs, zs, n, total,
-    pos_ref, vel_ref, mass_ref, tan_ref,
+    pos_hbm, vel_hbm, mass_hbm, tan_hbm,
     gram_ref, mat_ref, npos_ref, nvel_ref,
+    pos_ref, vel_ref, mass_ref, tan_ref, in_sem,
     row_z, row_p, dx_buf, src, tgt, k_hi, k_lo, dx_b,
     ext_send, ext_recv, out_send, out_recv,
-    g_own, g_sib, g_half, g_plane, g_mine, g_line, g_all,
+    g_own, g_plane, g_mine, g_line, g_all,
     pz_send, pz_recv, pp_send, pp_recv, ps_send, ps_recv,
-    up_send, up_recv, dn_send, dn_recv, sh_send, sh_recv,
+    hop_send, hop_recv, sh_send, sh_recv,
     ex_send, ex_recv, rs_send, rs_recv, gs_send, gs_recv,
 ):
     blk, lane = lax.axis_index("blk"), lax.axis_index("lane")
@@ -56,14 +66,22 @@
     planes = xs * Y
     targets = planes * n
     sources = 2 * zs * n
-    up_steps, dn_steps = zs // 2, (zs - 1) // 2
-
-    def plane_peer(i, j):
+    passes, phases = RING[zs]
+
+    def plane_peer(i, j, other=0):
         ox, oy = lax.rem(px + i, xs), lax.rem(py + j, Y)
-        return (ox * 4 + lax.rem(oy, 2) * 2 + core, z * 2 + oy // 2), ox * Y + oy
+        there = 1 - core if other else core
+        return (ox * 4 + lax.rem(oy, 2) * 2 + there, z * 2 + oy // 2), ox * Y + oy, there
 
     def plane_back(i, j):
         return lax.rem(xs - i, xs) * Y + lax.rem(Y - j, Y)
+
+    def away(length, r):
+        return min(r, length - r)
+
+    line = sorted(range(1, zs), key=lambda r: -away(zs, r))
+    plane = sorted(range(1, planes), key=lambda t: -away(xs, t // Y) - away(Y, t % Y))
+    both = [(t, other) for t in plane for other in range(2)] + [(0, 1)]
 
     def line_peer(r):
         return (blk, lax.rem(z + r, zs) * 2 + lax.rem(lane, 2))
@@ -77,66 +95,75 @@
             device_id=device, device_id_type=MESH,
         )
 
+    loads = [
+        pltpu.make_async_copy(source, target, in_sem.at[index])
+        for index, (source, target) in enumerate(
+            [(pos_hbm, pos_ref), (vel_hbm, vel_ref), (mass_hbm, mass_ref), (tan_hbm, tan_ref)]
+        )
+    ]
+    for load in loads:
+        load.start()
     barrier = pltpu.get_barrier_semaphore()
-    for r in range(1, zs):
+    for r in line:
         pl.semaphore_signal(barrier, inc=1, device_id=line_peer(r), device_id_type=MESH)
-    for t in range(1, planes):
-        pl.semaphore_signal(barrier, inc=1, device_id=plane_peer(t // Y, t % Y)[0], device_id_type=MESH)
-    pl.semaphore_signal(barrier, inc=1, device_id=sibling, device_id_type=MESH)
-
+    for t, other in both:
+        pl.semaphore_signal(barrier, inc=1, device_id=plane_peer(t // Y, t % Y, other)[0], device_id_type=MESH)
+
+    for load in loads:
+        load.wait()
     pos_half = pos_ref[...] + HALF * vel_ref[...]
-    row_z[0, 0] = jnp.zeros((8, 128), jnp.float32)
+    row_z[0, 0] = jnp.zeros((4, 128), jnp.float32)
     row_z[0, 0, 0:3, 0:n] = pos_half
     row_z[0, 0, 3:4, 0:n] = mass_ref[...] / total
     row_p[0] = row_z[0, 0]
     dx_half = tan_ref[0:3] + HALF * tan_ref[3:6]
     dx_buf[:, 0, 0] = dx_half
-    pl.semaphore_wait(barrier, zs - 1 + planes - 1 + 1)
-
-    for r in range(1, zs):
+    pl.semaphore_wait(barrier, zs - 1 + 2 * planes - 1)
+
+    pending = []
+    for r in line:
         remote(row_z.at[0, 0], row_z.at[0, zs - r], pz_send, pz_recv, line_peer(r)).start()
-    for t in range(1, planes):
+    for t in plane:
         remote(row_z.at[0, 0], row_p.at[plane_back(t // Y, t % Y)], pp_send, pp_recv, plane_peer(t // Y, t % Y)[0]).start()
 
-    def up_copy(s):
+    line_slots, plane_slots = row_z.at[0, pl.ds(1, zs - 1)], row_p.at[pl.ds(1, planes - 1)]
+    line_all = remote(line_slots, line_slots, pz_send, pz_recv, sibling)
+    plane_all = remote(plane_slots, plane_slots, pp_send, pp_recv, sibling)
+    pending += [line_all.wait_send, plane_all.wait_send]
+
+    def begin(copy):
+        copy.start()
+        pending.append(copy.wait_send)
+
+    def hop(start, end):
         return remote(
-            dx_buf.at[:, 0, (zs - s + 1) % zs], dx_buf.at[:, 0, zs - s],
-            up_send.at[s - 1], up_recv.at[s - 1], line_peer(1),
+            dx_buf.at[:, 0, -start % zs], dx_buf.at[:, 0, -end % zs],
+            hop_send.at[end % zs], hop_recv.at[end % zs], line_peer((end - start) % zs),
         )
 
-    def dn_copy(s):
-        return remote(
-            dx_buf.at[:, 0, s - 1], dx_buf.at[:, 0, s],
-            dn_send.at[s - 1], dn_recv.at[s - 1], line_peer(zs - 1),
-        )
+    before = {end: start for start, ends in passes.items() for end in ends}
 
     def share(r):
         return remote(dx_buf.at[:, 0, r], dx_buf.at[:, 1, r], sh_send.at[r], sh_recv.at[r], sibling)
 
-    def advance(s):
-        up_copy(s).wait_recv()
-        if s + 1 <= up_steps:
-            up_copy(s + 1).start()
-        if s <= dn_steps:
-            dn_copy(s).wait_recv()
-            if s + 1 <= dn_steps:
-                dn_copy(s + 1).start()
-        share(zs - s).start()
-        if s <= dn_steps:
-            share(s).start()
-
-    up_copy(1).start()
-    if dn_steps:
-        dn_copy(1).start()
-    share(0).start()
-
-    remote(row_z.at[0, pl.ds(1, zs - 1)], row_z.at[0, pl.ds(1, zs - 1)], pz_send, pz_recv, sibling).wait_recv()
+    def visit(place):
+        if place:
+            hop(before[place], place).wait_recv()
+        for end in passes.get(place, ()):
+            begin(hop(place, end))
+        begin(share(-place % zs))
+
+    visit(0)
+    for place in phases[0]:
+        visit(place)
+    line_all.wait_recv()
     line_share = remote(row_z.at[0], row_z.at[1], ps_send, ps_recv, sibling)
-    line_share.start()
-    remote(row_p.at[pl.ds(1, planes - 1)], row_p.at[pl.ds(1, planes - 1)], pp_send, pp_recv, sibling).wait_recv()
+    begin(line_share)
+    plane_all.wait_recv()
     for c, piece in enumerate(pack_lanes([row_p[t] for t in range(planes)], n)):
-        tgt[c * 128:(c + 1) * 128, 0:8] = piece.T
-    advance(1)
+        tgt[c * 128:(c + 1) * 128, 0:8] = jnp.concatenate([piece, piece], axis=0).T
+    for place in phases[1]:
+        visit(place)
     line_share.wait_recv()
     tiles = [row_z[h, r] for h in range(2) for r in range(zs)]
     for c, piece in enumerate(pack_lanes(tiles, n)):
@@ -182,20 +209,20 @@
         return 0
 
     blocks = targets // 16
-    slots = max(up_steps - 1, 1)
-    done = 0
-    for s in range(2, up_steps + 1):
-        upto = blocks * (s - 1) // slots
-        lax.fori_loop(done, upto, pair_block, 0)
-        done = upto
-        advance(s)
-
-    for t in range(1, planes):
+    most = blocks * 5 // 8
+    lax.fori_loop(0, most, pair_block, 0)
+    for place in phases[2]:
+        visit(place)
+    lax.fori_loop(most, blocks, pair_block, 0)
+
+    for t in plane:
         back = plane_back(t // Y, t % Y)
         remote(
             ext_send.at[pl.ds(t * n, n)], ext_recv.at[back - 1], ex_send, ex_recv, plane_peer(t // Y, t % Y)[0]
         ).start()
 
+    ext_all = remote(ext_recv, ext_recv, ex_send, ex_recv, sibling)
+    pending.append(ext_all.wait_send)
     for r in range(zs):
         share(r).wait_recv()
     for b in range(3):
@@ -210,13 +237,14 @@
     group = 4
     rows = group * 3 * n
 
-    def pull_group(g, _):
+    def pull_group(step, _):
+        g = jnp.where(step < 2, step + 2, 3 - step) if xs == 4 else step
         where = pl.ds(pl.multiple_of(g * rows, 16), rows)
         first = jnp.dot(k_hi[where, :], dx_b[...], preferred_element_type=jnp.float32)
         second = jnp.dot(k_lo[where, :], dx_b[:, 0:128], preferred_element_type=jnp.float32)
         pulled = first[:, 0:128] + (first[:, 128:256] + second)
         out_send[pl.ds(g * (group // 2), group // 2)] = pulled.reshape(group // 2, 3, 2, n, 128)
-        for u in range(group):
+        for u in (2, 1, 3, 0):
             t = g * group + u
             i, j = t // Y, lax.rem(t, Y)
 
@@ -231,7 +259,9 @@
 
     lax.fori_loop(0, planes // group, pull_group, 0)
 
-    remote(ext_recv, ext_recv, ex_send, ex_recv, sibling).wait_recv()
+    out_all = remote(out_recv, out_recv, rs_send, rs_recv, sibling)
+    pending.append(out_all.wait_send)
+    ext_all.wait_recv()
     extra = ext_send[0:n, :]
     for t in range(planes - 1):
         extra = extra + ext_recv[t]
@@ -250,7 +280,7 @@
             taken = taken + extra[:, index[a, e]:index[a, e] + 1] * dx_buf[e, 0, 0]
         offset.append(taken)
 
-    remote(out_recv, out_recv, rs_send, rs_recv, sibling).wait_recv()
+    out_all.wait_recv()
     for a in range(3):
         pulled = out_send[0, a, 0]
         for t in range(planes - 1):
@@ -264,54 +294,41 @@
     )
 
     part_rows = 64 // planes
-    g_own[...] = gram.reshape(2, planes, part_rows, 128)
-    first = remote(g_own.at[1 - core], g_sib, gs_send.at[0], gs_recv.at[0], sibling)
-    first.start()
-    first.wait_recv()
-    g_half[...] = g_own[core] + g_sib[...]
-    for t in range(1, planes):
-        device, place = plane_peer(t // Y, t % Y)
+    g_own[...] = gram.reshape(2 * planes, part_rows, 128)
+    for t, other in both:
+        device, place, there = plane_peer(t // Y, t % Y, other)
         remote(
-            g_half.at[place], g_plane.at[plane_back(t // Y, t % Y) - 1], gs_send.at[1], gs_recv.at[1], device
+            g_own.at[there * planes + place], g_plane.at[plane_back(t // Y, t % Y) * 2 + other - 1],
+            gs_send.at[0], gs_recv.at[0], device,
         ).start()
-    remote(g_plane, g_plane, gs_send.at[1], gs_recv.at[1], sibling).wait_recv()
-    mine = g_half[here]
-    for t in range(planes - 1):
+    plane_sums = remote(g_plane, g_plane, gs_send.at[0], gs_recv.at[0], sibling)
+    pending.append(plane_sums.wait_send)
+    plane_sums.wait_recv()
+    own = core * planes + here
+    mine = g_own[own]
+    for t in range(2 * planes - 1):
         mine = mine + g_plane[t]
     g_mine[...] = mine
-    for r in range(1, zs):
-        remote(g_mine, g_line.at[zs - r - 1], gs_send.at[2], gs_recv.at[2], line_peer(r)).start()
-    remote(g_line, g_line, gs_send.at[2], gs_recv.at[2], sibling).wait_recv()
+    for r in line:
+        remote(g_mine, g_line.at[zs - r - 1], gs_send.at[1], gs_recv.at[1], line_peer(r)).start()
+    line_sums = remote(g_line, g_line, gs_send.at[1], gs_recv.at[1], sibling)
+    pending.append(line_sums.wait_send)
+    line_sums.wait_recv()
     for r in range(zs - 1):
         mine = mine + g_line[r]
-    g_all[core, here] = mine / (6.0 * total)
-    for t in range(1, planes):
+    g_all[own] = mine / (6.0 * total)
+    for t, other in both:
         remote(
-            g_all.at[core, here], g_all.at[core, here], gs_send.at[3], gs_recv.at[3], plane_peer(t // Y, t % Y)[0]
+            g_all.at[own], g_all.at[own], gs_send.at[2], gs_recv.at[2], plane_peer(t // Y, t % Y, other)[0]
         ).start()
-    some = g_all.at[core, pl.ds(0, planes - 1)]
-    remote(some, some, gs_send.at[3], gs_recv.at[3], sibling).wait_recv()
-    last = remote(g_all.at[core], g_all.at[core], gs_send.at[4], gs_recv.at[4], sibling)
-    last.start()
-    last.wait_recv()
+    whole = g_all.at[pl.ds(0, 2 * planes - 1)]
+    whole = remote(whole, whole, gs_send.at[2], gs_recv.at[2], sibling)
+    pending.append(whole.wait_send)
+    whole.wait_recv()
     gram_ref[...] = g_all[...].reshape(128, 128)
 
-    remote(row_z.at[0, pl.ds(1, zs - 1)], row_z.at[0, pl.ds(1, zs - 1)], pz_send, pz_recv, sibling).wait_send()
-    remote(row_p.at[pl.ds(1, planes - 1)], row_p.at[pl.ds(1, planes - 1)], pp_send, pp_recv, sibling).wait_send()
-    line_share.wait_send()
-    for s in range(1, up_steps + 1):
-        up_copy(s).wait_send()
-        if s <= dn_steps:
-            dn_copy(s).wait_send()
-    for r in range(zs):
-        share(r).wait_send()
-    remote(ext_recv, ext_recv, ex_send, ex_recv, sibling).wait_send()
-    remote(out_recv, out_recv, rs_send, rs_recv, sibling).wait_send()
-    first.wait_send()
-    remote(g_plane, g_plane, gs_send.at[1], gs_recv.at[1], sibling).wait_send()
-    remote(g_line, g_line, gs_send.at[2], gs_recv.at[2], sibling).wait_send()
-    remote(some, some, gs_send.at[3], gs_recv.at[3], sibling).wait_send()
-    last.wait_send()
+    for wait in pending:
+        wait()
 
 
 def factor_kernel(gram_ref, mat_ref, npos_ref, nvel_ref, pos_out, vel_out, basis_out, growth_out):
@@ -365,10 +382,15 @@
     dma = pltpu.SemaphoreType.DMA
     part_rows = 64 // planes
     scratch = [
-        pltpu.VMEM((2, zs, 8, 128), f32),
-        pltpu.VMEM((planes, 8, 128), f32),
+        pltpu.VMEM((3, n), f32),
+        pltpu.VMEM((3, n), f32),
+        pltpu.VMEM((1, n), f32),
+        pltpu.VMEM((6, n, k), f32),
+        dma((4,)),
+        pltpu.VMEM((2, zs, 4, 128), f32),
+        pltpu.VMEM((planes, 4, 128), f32),
         pltpu.VMEM((3, 2, zs, n, k), f32),
-        pltpu.VMEM((8, sources), f32),
+        pltpu.VMEM((4, sources), f32),
         pltpu.VMEM(((targets + 127) // 128 * 128, 128), f32),
         pltpu.VMEM((3 * targets, 3 * sources), bf16),
         pltpu.VMEM((3 * targets, 3 * sources), bf16),
@@ -377,17 +399,15 @@
         pltpu.VMEM((planes - 1, n, 128), f32),
         pltpu.VMEM((planes // 2, 3, 2, n, k), f32),
         pltpu.VMEM((planes - 1, 3, n, k), f32),
-        pltpu.VMEM((2, planes, part_rows, k), f32),
-        pltpu.VMEM((planes, part_rows, k), f32),
-        pltpu.VMEM((planes, part_rows, k), f32),
-        pltpu.VMEM((planes - 1, part_rows, k), f32),
+        pltpu.VMEM((2 * planes, part_rows, k), f32),
+        pltpu.VMEM((2 * planes - 1, part_rows, k), f32),
         pltpu.VMEM((part_rows, k), f32),
         pltpu.VMEM((zs - 1, part_rows, k), f32),
-        pltpu.VMEM((2, planes, part_rows, k), f32),
+        pltpu.VMEM((2 * planes, part_rows, k), f32),
         dma, dma, dma, dma, dma, dma,
-        dma((zs // 2,)), dma((zs // 2,)), dma((zs // 2,)), dma((zs // 2,)),
         dma((zs,)), dma((zs,)),
-        dma, dma, dma, dma, dma((5,)), dma((5,)),
+        dma((zs,)), dma((zs,)),
+        dma, dma, dma, dma, dma((3,)), dma((3,)),
     ]
     gram, matrix, npos, nvel = pl.pallas_call(
         functools.partial(step_kernel, xs, zs, n, total),
@@ -397,13 +417,16 @@
             jax.ShapeDtypeStruct((3, n), f32),
             jax.ShapeDtypeStruct((3, n), f32),
         ],
-        in_specs=[vmem] * 4,
+        in_specs=[pl.BlockSpec(memory_space=pltpu.HBM)] * 4,
         out_specs=[vmem] * 4,
         scratch_shapes=scratch,
         compiler_params=pltpu.CompilerParams(
             collective_id=0, has_side_effects=True, vmem_limit_bytes=40 * 1024 * 1024
         ),
-    )(positions, velocities, masses.reshape(1, n), tangents)
+    )(*[
+        pltpu.with_memory_space_constraint(array, pltpu.HBM)
+        for array in (positions, velocities, masses.reshape(1, n), tangents)
+    ])
     npos, nvel, basis, growth = pl.pallas_call(
         factor_kernel,
         out_shape=[

time: 88.9 us -> 70.1 us (0.79)
  Pallas kernels: 85.1 us -> 69.3 us
  local copies, waits for them, and re-layouts: 2.89 us -> 0 us
    pallas_call x1, Pallas kernels: 80.2 us -> 64.3 us  [body(): pl.pallas_call(functools.partial(step_kernel, xs, zs, n, total), out_shap...]
    unnamed x8 -> x0, local copies, waits for them, and re-layouts: 2.89 us -> none
where the time goes in v2:
time: 70.1 us; the launch traced here: 69.9 us
  Pallas kernels  69.3 us (99%)
    pallas_call x1, Pallas kernels, body(): pl.pallas_call(functools.partial(step_kernel, xs, zs, n, total), out_shap...  64.3 us
    pallas_call x1, Pallas kernels, body(): pl.pallas_call(factor_kernel, out_shape=[jax.ShapeDtypeStruct((3, n), f32...  4.92 us

profile of v2, /device:TPU:1, one launch (start us, length us, event | category | flops | bytes accessed | tf_op | source)
XLA Modules:
  0.0 69.9 jit_solution(11156297384245469528)
XLA Ops:
  0.6 64.3 %shard_map.75 = (f32[128,128]{1,0:T(8,128)S(1)}, f32[6,24,128]{2,1,0:T(8,128)S(1)}, f32[3,24]{1,0:T(4,128)S(1)}, f32[3,24]{1,0:T(4,128)S(1)}) custom-call(f32[3,24]{1,0:T(4,128)} %pos_hbm.1, f32[3,24]{1,0:T(4,128)} %vel_hbm.1, f32[1,24]{1,0:T(1,128)} %bitcast.1, f32[6,24,128]{2,1,0:T(8,128)} %tan_hbm.1), custom_call_target="tpu_custom_call" | custom-call | tf_op jit(solution)/shard_map/pallas_call | solution.py:412
  65.0 4.9 %shard_map.76 = (f32[3,24]{1,0:T(4,128)}, f32[3,24]{1,0:T(4,128)}, f32[6,24,128]{2,1,0:T(8,128)}, f32[128,128]{1,0:T(8,128)}) custom-call(f32[128,128]{1,0:T(8,128)S(1)} %get-tuple-element.8.gram_ref, f32[6,24,128]{2,1,0:T(8,128)S(1)} %get-tuple-element.9.mat_ref, f32[3,24]{1,0:T(4,128)S(1)} %get-tuple-element.10.npos_ref, ...), custom_call_target="tpu_custom_call" | custom-call | tf_op jit(solution)/shard_map/pallas_call | solution.py:430

commit v3 on v2

--- a/solution.py
+++ b/solution.py
@@ -18,9 +18,10 @@
 RING = {
     16: (
         {0: (3, -3, 1, -1), 3: (6, 2, 4), -3: (-6, -2, -4), 6: (8, 5, 7), -6: (-5, -7)},
-        ((3, -3, 1, -1), (6, -6, 2, -2, 4, -4), (5, -5, 7, -7, 8)),
+        ((0, 3, -3, 1, -1), (6, -6, 2, -2, 4, -4), (5, -5, 7, -7, 8)),
+        3,
     ),
-    4: ({0: (1, -1), 1: (2,)}, ((1,), (-1,), (2,))),
+    4: ({0: (1, -1), 1: (2,)}, ((0, 1), (-1,), (2,)), 1),
 }
 
 
@@ -28,22 +29,16 @@
     return lax.broadcasted_iota(jnp.int32, shape, 1)
 
 
-def pack_lanes(tiles, width):
-    pieces = [None] * ((len(tiles) * width + 127) // 128)
+def pack_lanes(tile_of, count, width, chunk):
     lanes = lane_iota((4, 128))
-
-    def put(index, value):
-        pieces[index] = value if pieces[index] is None else pieces[index] + value
-
-    for index, tile in enumerate(tiles):
-        chunk, offset = divmod(index * width, 128)
-        turned = pltpu.roll(tile, offset, 1) if offset else tile
+    total = jnp.zeros((4, 128), jnp.float32)
+    for index in range(128 * chunk // width, min(count, (128 * chunk + 127) // width + 1)):
+        first, offset = divmod(index * width, 128)
+        turned = pltpu.roll(tile_of(index), offset, 1) if offset else tile_of(index)
         if offset + width > 128:
-            put(chunk, jnp.where(lanes >= offset, turned, 0.0))
-            put(chunk + 1, jnp.where(lanes < offset, turned, 0.0))
-        else:
-            put(chunk, turned)
-    return pieces
+            turned = jnp.where((lanes >= offset) if first == chunk else (lanes < offset), turned, 0.0)
+        total = total + turned
+    return total
 
 
 def step_kernel(
@@ -51,10 +46,10 @@
     pos_hbm, vel_hbm, mass_hbm, tan_hbm,
     gram_ref, mat_ref, npos_ref, nvel_ref,
     pos_ref, vel_ref, mass_ref, tan_ref, in_sem,
-    row_z, row_p, dx_buf, src, tgt, k_hi, k_lo, dx_b,
-    ext_send, ext_recv, out_send, out_recv,
+    row_p, dx_buf, src, tgt, k_hi, k_lo, dx_b,
+    ext_all_rows, ext_send, ext_recv, out_send, out_recv,
     g_own, g_plane, g_mine, g_line, g_all,
-    pz_send, pz_recv, pp_send, pp_recv, ps_send, ps_recv,
+    pp_send, pp_recv,
     hop_send, hop_recv, sh_send, sh_recv,
     ex_send, ex_recv, rs_send, rs_recv, gs_send, gs_recv,
 ):
@@ -66,7 +61,14 @@
     planes = xs * Y
     targets = planes * n
     sources = 2 * zs * n
-    passes, phases = RING[zs]
+    passes, phases, reach = RING[zs]
+    order = [(h, place) for group in phases for h in range(2) for place in group]
+    early = 2 * (len(phases[0]) + len(phases[1])) * n // 128
+    split = 3 * 128 * early
+    width = sources // 128 - early
+
+    def column(b, chunk):
+        return 128 * (b * early + chunk) if chunk < early else split + 128 * (b * width + chunk - early)
 
     def plane_peer(i, j, other=0):
         ox, oy = lax.rem(px + i, xs), lax.rem(py + j, Y)
@@ -104,32 +106,28 @@
     for load in loads:
         load.start()
     barrier = pltpu.get_barrier_semaphore()
-    for r in line:
+    near = sorted({r % zs for r in range(-reach, reach + 1)} - {0}, key=lambda r: -away(zs, r))
+    for r in near:
         pl.semaphore_signal(barrier, inc=1, device_id=line_peer(r), device_id_type=MESH)
-    for t, other in both:
-        pl.semaphore_signal(barrier, inc=1, device_id=plane_peer(t // Y, t % Y, other)[0], device_id_type=MESH)
+    for t in plane:
+        pl.semaphore_signal(barrier, inc=1, device_id=plane_peer(t // Y, t % Y)[0], device_id_type=MESH)
+    pl.semaphore_signal(barrier, inc=1, device_id=sibling, device_id_type=MESH)
 
     for load in loads:
         load.wait()
     pos_half = pos_ref[...] + HALF * vel_ref[...]
-    row_z[0, 0] = jnp.zeros((4, 128), jnp.float32)
-    row_z[0, 0, 0:3, 0:n] = pos_half
-    row_z[0, 0, 3:4, 0:n] = mass_ref[...] / total
-    row_p[0] = row_z[0, 0]
+    row_p[0] = jnp.zeros((4, 128), jnp.float32)
+    row_p[0, 0:3, 0:n] = pos_half
+    row_p[0, 3:4, 0:n] = mass_ref[...] / total
     dx_half = tan_ref[0:3] + HALF * tan_ref[3:6]
-    dx_buf[:, 0, 0] = dx_half
-    pl.semaphore_wait(barrier, zs - 1 + 2 * planes - 1)
+    dx_buf[0, 0, 0:3 * n] = dx_half.reshape(3 * n, 128)
+    dx_buf[0, 0, 3 * n:3 * n + 4] = row_p[0]
+    dx_buf[0, 0, 3 * n + 4:3 * n + 8] = jnp.zeros((4, 128), jnp.float32)
+    pl.semaphore_wait(barrier, len(near) + planes)
 
     pending = []
-    for r in line:
-        remote(row_z.at[0, 0], row_z.at[0, zs - r], pz_send, pz_recv, line_peer(r)).start()
-    for t in plane:
-        remote(row_z.at[0, 0], row_p.at[plane_back(t // Y, t % Y)], pp_send, pp_recv, plane_peer(t // Y, t % Y)[0]).start()
-
-    line_slots, plane_slots = row_z.at[0, pl.ds(1, zs - 1)], row_p.at[pl.ds(1, planes - 1)]
-    line_all = remote(line_slots, line_slots, pz_send, pz_recv, sibling)
+    plane_slots = row_p.at[pl.ds(1, planes - 1)]
     plane_all = remote(plane_slots, plane_slots, pp_send, pp_recv, sibling)
-    pending += [line_all.wait_send, plane_all.wait_send]
 
     def begin(copy):
         copy.start()
@@ -137,14 +135,14 @@
 
     def hop(start, end):
         return remote(
-            dx_buf.at[:, 0, -start % zs], dx_buf.at[:, 0, -end % zs],
+            dx_buf.at[0, -start % zs], dx_buf.at[0, -end % zs],
             hop_send.at[end % zs], hop_recv.at[end % zs], line_peer((end - start) % zs),
         )
 
     before = {end: start for start, ends in passes.items() for end in ends}
 
     def share(r):
-        return remote(dx_buf.at[:, 0, r], dx_buf.at[:, 1, r], sh_send.at[r], sh_recv.at[r], sibling)
+        return remote(dx_buf.at[0, r], dx_buf.at[1, r], sh_send.at[r], sh_recv.at[r], sibling)
 
     def visit(place):
         if place:
@@ -153,32 +151,38 @@
             begin(hop(place, end))
         begin(share(-place % zs))
 
+    def joined(group):
+        for place in group:
+            share(-place % zs).wait_recv()
+
+    def pack_sources(chunks):
+        def tile_of(q):
+            h, place = order[q]
+            return dx_buf[h, -place % zs, 3 * n:3 * n + 4, :]
+
+        for chunk in chunks:
+            src[:, 128 * chunk:128 * chunk + 128] = pack_lanes(tile_of, 2 * zs, n, chunk)
+
     visit(0)
-    for place in phases[0]:
+    for t in plane:
+        remote(row_p.at[0], row_p.at[plane_back(t // Y, t % Y)], pp_send, pp_recv, plane_peer(t // Y, t % Y)[0]).start()
+    pending.append(plane_all.wait_send)
+    for place in phases[0][1:]:
         visit(place)
-    line_all.wait_recv()
-    line_share = remote(row_z.at[0], row_z.at[1], ps_send, ps_recv, sibling)
-    begin(line_share)
     plane_all.wait_recv()
-    for c, piece in enumerate(pack_lanes([row_p[t] for t in range(planes)], n)):
+    for c in range((targets + 127) // 128):
+        piece = pack_lanes(lambda t: row_p[t], planes, n, c)
         tgt[c * 128:(c + 1) * 128, 0:8] = jnp.concatenate([piece, piece], axis=0).T
-    for place in phases[1]:
-        visit(place)
-    line_share.wait_recv()
-    tiles = [row_z[h, r] for h in range(2) for r in range(zs)]
-    for c, piece in enumerate(pack_lanes(tiles, n)):
-        src[:, c * 128:(c + 1) * 128] = piece
-
     subs = 2 * n // 16
     lanes16 = lane_iota((16, 128))
 
-    def pair_block(b, _):
+    def pair_block(chunks, b, _):
         pair, sub = b // subs, lax.rem(b, subs)
         base = pair * (6 * n) + sub * 16
         place = tgt[pl.ds(pl.multiple_of(b * 16, 16), 16), 0:8]
         own = [jnp.broadcast_to(place[:, a:a + 1], (16, 128)) for a in range(3)]
         sums = [None] * 9
-        for c in range(sources // 128):
+        for c in chunks:
             columns = pl.ds(c * 128, 128)
             d = [src[a:a + 1, columns] - own[a] for a in range(3)]
             squared = d[0] * d[0] + d[1] * d[1] + d[2] * d[2] + SOFT
@@ -199,51 +203,94 @@
                     high = part[a, e].astype(jnp.bfloat16)
                     low = (part[a, e] - high.astype(jnp.float32)).astype(jnp.bfloat16)
                     for f, g in {(a, e), (e, a)}:
-                        where = (pl.ds(pl.multiple_of(base + f * 2 * n, 16), 16), pl.ds(g * sources + c * 128, 128))
+                        where = (pl.ds(pl.multiple_of(base + f * 2 * n, 16), 16), pl.ds(column(g, c), 128))
                         k_hi[where] = high
                         k_lo[where] = low
         tile = jnp.zeros((16, 128), jnp.float32)
         for k, s in enumerate(sums):
             tile = jnp.where(lanes16 == k, jnp.sum(s, axis=1, keepdims=True), tile)
-        ext_send[pl.ds(pl.multiple_of(b * 16, 16), 16), :] = tile
+        where = pl.ds(pl.multiple_of(b * 16, 16), 16)
+        ext_all_rows[where, :] = tile if chunks[0] == 0 else ext_all_rows[where, :] + tile
         return 0
 
-    blocks = targets // 16
-    most = blocks * 5 // 8
-    lax.fori_loop(0, most, pair_block, 0)
+    progress = [0, 0]
+
+    def take(count):
+        chunks = range(progress[0], count * n // 128)
+        if len(chunks):
+            progress[0] = chunks[-1] + 1
+            pack_sources(chunks)
+            lax.fori_loop(0, targets // 16, functools.partial(pair_block, list(chunks)), 0)
+
+    def halves(count):
+        for q in range(progress[1], count, 2):
+            for b in range(3):
+                block = jnp.concatenate(
+                    [dx_buf[h, -place % zs, b * n:(b + 1) * n, :] for h, place in order[q:q + 2]], axis=0
+                )
+                first = q * n
+                while first < (q + 2) * n:
+                    last = min((q + 2) * n, first // 128 * 128 + 128)
+                    part = block[first - q * n:last - q * n, :]
+                    high = part.astype(jnp.bfloat16)
+                    low = (part - high.astype(jnp.float32)).astype(jnp.bfloat16)
+                    start = column(b, first // 128) + first % 128
+                    dx_b[start:start + last - first, 0:128] = high
+                    dx_b[start:start + last - first, 128:256] = low
+                    first = last
+        progress[1] = count
+
+    group = 4
+    rows = group * 3 * n
+
+    def pull(g, low, high):
+        where = pl.ds(pl.multiple_of(g * rows, 16), rows)
+        first = jnp.dot(k_hi[where, low:high], dx_b[low:high, :], preferred_element_type=jnp.float32)
+        second = jnp.dot(k_lo[where, low:high], dx_b[low:high, 0:128], preferred_element_type=jnp.float32)
+        pulled = first[:, 0:128] + (first[:, 128:256] + second)
+        return pulled.reshape(group // 2, 3, 2, n, 128)
+
+    def early_group(g, _):
+        out_send[pl.ds(g * (group // 2), group // 2)] = pull(g, 0, split)
+        return 0
+
+    joined(phases[0])
+    count = 2 * len(phases[0])
+    take(count)
+    for place in phases[1]:
+        visit(place)
+    joined(phases[1])
+    count += 2 * len(phases[1])
+    take(count)
     for place in phases[2]:
         visit(place)
-    lax.fori_loop(most, blocks, pair_block, 0)
-
+    halves(count)
+    if early:
+        lax.fori_loop(0, planes // group, early_group, 0)
+    take(count + len(phases[2]))
+    joined(phases[2])
+    take(2 * zs)
+
+    for t in range(planes):
+        tile = ext_all_rows[t * n:t * n + 8, :]
+        for u in range(1, n // 8):
+            tile = tile + pltpu.roll(ext_all_rows[t * n + 8 * u:t * n + 8 * u + 8, :], 16 * u, 1)
+        ext_send[t] = tile
     for t in plane:
         back = plane_back(t // Y, t % Y)
         remote(
-            ext_send.at[pl.ds(t * n, n)], ext_recv.at[back - 1], ex_send, ex_recv, plane_peer(t // Y, t % Y)[0]
+            ext_send.at[t], ext_recv.at[back - 1], ex_send, ex_recv, plane_peer(t // Y, t % Y)[0]
         ).start()
 
     ext_all = remote(ext_recv, ext_recv, ex_send, ex_recv, sibling)
     pending.append(ext_all.wait_send)
-    for r in range(zs):
-        share(r).wait_recv()
-    for b in range(3):
-        for h in range(2):
-            block = dx_buf[b, h].reshape(zs * n, 128)
-            high = block.astype(jnp.bfloat16)
-            low = (block - high.astype(jnp.float32)).astype(jnp.bfloat16)
-            start = b * sources + h * zs * n
-            dx_b[start:start + zs * n, 0:128] = high
-            dx_b[start:start + zs * n, 128:256] = low
-
-    group = 4
-    rows = group * 3 * n
+    halves(2 * zs)
 
     def pull_group(step, _):
         g = jnp.where(step < 2, step + 2, 3 - step) if xs == 4 else step
-        where = pl.ds(pl.multiple_of(g * rows, 16), rows)
-        first = jnp.dot(k_hi[where, :], dx_b[...], preferred_element_type=jnp.float32)
-        second = jnp.dot(k_lo[where, :], dx_b[:, 0:128], preferred_element_type=jnp.float32)
-        pulled = first[:, 0:128] + (first[:, 128:256] + second)
-        out_send[pl.ds(g * (group // 2), group // 2)] = pulled.reshape(group // 2, 3, 2, n, 128)
+        half = pl.ds(g * (group // 2), group // 2)
+        pulled = pull(g, split, 3 * sources)
+        out_send[half] = out_send[half] + pulled if early else pulled
         for u in (2, 1, 3, 0):
             t = g * group + u
             i, j = t // Y, lax.rem(t, Y)
@@ -262,9 +309,12 @@
     out_all = remote(out_recv, out_recv, rs_send, rs_recv, sibling)
     pending.append(out_all.wait_send)
     ext_all.wait_recv()
-    extra = ext_send[0:n, :]
+    extra = ext_send[0]
     for t in range(planes - 1):
         extra = extra + ext_recv[t]
+    extra = jnp.concatenate(
+        [pltpu.roll(extra, 128 - 16 * u, 1) if u else extra for u in range(n // 8)], axis=0
+    )
     acceleration = extra.T[0:3, :]
     new_velocities = vel_ref[...] + STEP * acceleration
     nvel_ref[...] = new_velocities
@@ -277,7 +327,7 @@
     for a in range(3):
         taken = 0.0
         for e in range(3):
-            taken = taken + extra[:, index[a, e]:index[a, e] + 1] * dx_buf[e, 0, 0]
+            taken = taken + extra[:, index[a, e]:index[a, e] + 1] * dx_buf[0, 0, e * n:(e + 1) * n, :]
         offset.append(taken)
 
     out_all.wait_recv()
@@ -287,7 +337,7 @@
             pulled = pulled + out_recv[t, a]
         dv_new = tan_ref[3 + a] + STEP * (pulled - offset[a])
         mat_ref[3 + a] = dv_new
-        mat_ref[a] = dx_buf[a, 0, 0] + HALF * dv_new
+        mat_ref[a] = dx_buf[0, 0, a * n:(a + 1) * n, :] + HALF * dv_new
     matrix = mat_ref[...].reshape(6 * n, 128)
     gram = lax.dot_general(
         matrix, matrix, (((0,), (0,)), ((), ())), precision=HIGHEST, preferred_element_type=jnp.float32
@@ -387,16 +437,16 @@
         pltpu.VMEM((1, n), f32),
         pltpu.VMEM((6, n, k), f32),
         dma((4,)),
-        pltpu.VMEM((2, zs, 4, 128), f32),
         pltpu.VMEM((planes, 4, 128), f32),
-        pltpu.VMEM((3, 2, zs, n, k), f32),
+        pltpu.VMEM((2, zs, 3 * n + 8, k), f32),
         pltpu.VMEM((4, sources), f32),
         pltpu.VMEM(((targets + 127) // 128 * 128, 128), f32),
         pltpu.VMEM((3 * targets, 3 * sources), bf16),
         pltpu.VMEM((3 * targets, 3 * sources), bf16),
         pltpu.VMEM((3 * sources, 2 * k), bf16),
         pltpu.VMEM((targets, 128), f32),
-        pltpu.VMEM((planes - 1, n, 128), f32),
+        pltpu.VMEM((planes, 8, 128), f32),
+        pltpu.VMEM((planes - 1, 8, 128), f32),
         pltpu.VMEM((planes // 2, 3, 2, n, k), f32),
         pltpu.VMEM((planes - 1, 3, n, k), f32),
         pltpu.VMEM((2 * planes, part_rows, k), f32),
@@ -404,7 +454,7 @@
         pltpu.VMEM((part_rows, k), f32),
         pltpu.VMEM((zs - 1, part_rows, k), f32),
         pltpu.VMEM((2 * planes, part_rows, k), f32),
-        dma, dma, dma, dma, dma, dma,
+        dma, dma,
         dma((zs,)), dma((zs,)),
         dma((zs,)), dma((zs,)),
         dma, dma, dma, dma, dma((3,)), dma((3,)),

time: 70.1 us -> 79.3 us (1.13)
  Pallas kernels: 69.3 us -> 78.5 us
    pallas_call x1, Pallas kernels: 64.3 us -> 73.6 us  [body(): pl.pallas_call(functools.partial(step_kernel, xs, zs, n, total), out_shap...]
where the time goes in v3:
time: 79.3 us; the launch traced here: 79.2 us
  Pallas kernels  78.5 us (99%)
    pallas_call x1, Pallas kernels, body(): pl.pallas_call(functools.partial(step_kernel, xs, zs, n, total), out_shap...  73.6 us
    pallas_call x1, Pallas kernels, body(): pl.pallas_call(factor_kernel, out_shape=[jax.ShapeDtypeStruct((3, n), f32...  4.92 us

profile of v3, /device:TPU:1, one launch (start us, length us, event | category | flops | bytes accessed | tf_op | source)
XLA Modules:
  0.0 79.2 jit_solution(5983709013081170866)
XLA Ops:
  0.6 73.6 %shard_map.75 = (f32[128,128]{1,0:T(8,128)S(1)}, f32[6,24,128]{2,1,0:T(8,128)S(1)}, f32[3,24]{1,0:T(4,128)S(1)}, f32[3,24]{1,0:T(4,128)S(1)}) custom-call(f32[3,24]{1,0:T(4,128)} %pos_hbm.1, f32[3,24]{1,0:T(4,128)} %vel_hbm.1, f32[1,24]{1,0:T(1,128)} %bitcast.1, f32[6,24,128]{2,1,0:T(8,128)} %tan_hbm.1), custom_call_target="tpu_custom_call" | custom-call | tf_op jit(solution)/shard_map/pallas_call | solution.py:462
  74.2 4.9 %shard_map.76 = (f32[3,24]{1,0:T(4,128)}, f32[3,24]{1,0:T(4,128)}, f32[6,24,128]{2,1,0:T(8,128)}, f32[128,128]{1,0:T(8,128)}) custom-call(f32[128,128]{1,0:T(8,128)S(1)} %get-tuple-element.8.gram_ref, f32[6,24,128]{2,1,0:T(8,128)S(1)} %get-tuple-element.9.mat_ref, f32[3,24]{1,0:T(4,128)S(1)} %get-tuple-element.10.npos_ref, ...), custom_call_target="tpu_custom_call" | custom-call | tf_op jit(solution)/shard_map/pallas_call | solution.py:480

commit v4 on v3

--- a/solution.py
+++ b/solution.py
@@ -47,7 +47,7 @@
     gram_ref, mat_ref, npos_ref, nvel_ref,
     pos_ref, vel_ref, mass_ref, tan_ref, in_sem,
     row_p, dx_buf, src, tgt, k_hi, k_lo, dx_b,
-    ext_all_rows, ext_send, ext_recv, out_send, out_recv,
+    lane_sums, ext_send, ext_recv, out_send, out_recv,
     g_own, g_plane, g_mine, g_line, g_all,
     pp_send, pp_recv,
     hop_send, hop_recv, sh_send, sh_recv,
@@ -172,16 +172,15 @@
     plane_all.wait_recv()
     for c in range((targets + 127) // 128):
         piece = pack_lanes(lambda t: row_p[t], planes, n, c)
-        tgt[c * 128:(c + 1) * 128, 0:8] = jnp.concatenate([piece, piece], axis=0).T
-    subs = 2 * n // 16
-    lanes16 = lane_iota((16, 128))
-
-    def pair_block(chunks, b, _):
-        pair, sub = b // subs, lax.rem(b, subs)
-        base = pair * (6 * n) + sub * 16
-        place = tgt[pl.ds(pl.multiple_of(b * 16, 16), 16), 0:8]
-        own = [jnp.broadcast_to(place[:, a:a + 1], (16, 128)) for a in range(3)]
-        sums = [None] * 9
+        columns = jnp.concatenate([piece, piece], axis=0).T
+        last = min(128, targets - c * 128)
+        for a in range(3):
+            tgt[a, c * 128:c * 128 + last, :] = jnp.broadcast_to(columns[0:last, a:a + 1], (last, 128))
+    def pair_block(chunks, pair, _):
+        where = pl.ds(pl.multiple_of(pair * 2 * n, 16), 2 * n)
+        base = pair * (6 * n)
+        own = [tgt[a, where, :] for a in range(3)]
+        sums = [None if chunks[0] == 0 else lane_sums[k, where, :] for k in range(9)]
         for c in chunks:
             columns = pl.ds(c * 128, 128)
             d = [src[a:a + 1, columns] - own[a] for a in range(3)]
@@ -203,14 +202,11 @@
                     high = part[a, e].astype(jnp.bfloat16)
                     low = (part[a, e] - high.astype(jnp.float32)).astype(jnp.bfloat16)
                     for f, g in {(a, e), (e, a)}:
-                        where = (pl.ds(pl.multiple_of(base + f * 2 * n, 16), 16), pl.ds(column(g, c), 128))
-                        k_hi[where] = high
-                        k_lo[where] = low
-        tile = jnp.zeros((16, 128), jnp.float32)
-        for k, s in enumerate(sums):
-            tile = jnp.where(lanes16 == k, jnp.sum(s, axis=1, keepdims=True), tile)
-        where = pl.ds(pl.multiple_of(b * 16, 16), 16)
-        ext_all_rows[where, :] = tile if chunks[0] == 0 else ext_all_rows[where, :] + tile
+                        to = (pl.ds(pl.multiple_of(base + f * 2 * n, 16), 2 * n), pl.ds(column(g, c), 128))
+                        k_hi[to] = high
+                        k_lo[to] = low
+        for k in range(9):
+            lane_sums[k, where, :] = sums[k]
         return 0
 
     progress = [0, 0]
@@ -220,7 +216,7 @@
         if len(chunks):
             progress[0] = chunks[-1] + 1
             pack_sources(chunks)
-            lax.fori_loop(0, targets // 16, functools.partial(pair_block, list(chunks)), 0)
+            lax.fori_loop(0, planes // 2, functools.partial(pair_block, list(chunks)), 0, unroll=2)
 
     def halves(count):
         for q in range(progress[1], count, 2):
@@ -271,19 +267,6 @@
     joined(phases[2])
     take(2 * zs)
 
-    for t in range(planes):
-        tile = ext_all_rows[t * n:t * n + 8, :]
-        for u in range(1, n // 8):
-            tile = tile + pltpu.roll(ext_all_rows[t * n + 8 * u:t * n + 8 * u + 8, :], 16 * u, 1)
-        ext_send[t] = tile
-    for t in plane:
-        back = plane_back(t // Y, t % Y)
-        remote(
-            ext_send.at[t], ext_recv.at[back - 1], ex_send, ex_recv, plane_peer(t // Y, t % Y)[0]
-        ).start()
-
-    ext_all = remote(ext_recv, ext_recv, ex_send, ex_recv, sibling)
-    pending.append(ext_all.wait_send)
     halves(2 * zs)
 
     def pull_group(step, _):
@@ -305,6 +288,22 @@
         return 0
 
     lax.fori_loop(0, planes // group, pull_group, 0)
+
+    lanes8 = lane_iota((8, 128))
+    for t in plane + [0]:
+        tile = jnp.zeros((8, 128), jnp.float32)
+        for u in range(n // 8):
+            for k in range(9):
+                total_k = jnp.sum(lane_sums[k, t * n + 8 * u:t * n + 8 * u + 8, :], axis=1, keepdims=True)
+                tile = jnp.where(lanes8 == 16 * u + k, total_k, tile)
+        ext_send[t] = tile
+        if t:
+            remote(
+                ext_send.at[t], ext_recv.at[plane_back(t // Y, t % Y) - 1], ex_send, ex_recv,
+                plane_peer(t // Y, t % Y)[0],
+            ).start()
+    ext_all = remote(ext_recv, ext_recv, ex_send, ex_recv, sibling)
+    pending.append(ext_all.wait_send)
 
     out_all = remote(out_recv, out_recv, rs_send, rs_recv, sibling)
     pending.append(out_all.wait_send)
@@ -440,11 +439,11 @@
         pltpu.VMEM((planes, 4, 128), f32),
         pltpu.VMEM((2, zs, 3 * n + 8, k), f32),
         pltpu.VMEM((4, sources), f32),
-        pltpu.VMEM(((targets + 127) // 128 * 128, 128), f32),
+        pltpu.VMEM((3, targets, 128), f32),
         pltpu.VMEM((3 * targets, 3 * sources), bf16),
         pltpu.VMEM((3 * targets, 3 * sources), bf16),
         pltpu.VMEM((3 * sources, 2 * k), bf16),
-        pltpu.VMEM((targets, 128), f32),
+        pltpu.VMEM((9, targets, 128), f32),
         pltpu.VMEM((planes, 8, 128), f32),
         pltpu.VMEM((planes - 1, 8, 128), f32),
         pltpu.VMEM((planes // 2, 3, 2, n, k), f32),

time: 79.3 us -> 69.1 us (0.87)
  Pallas kernels: 78.5 us -> 68.3 us
    pallas_call x1, Pallas kernels: 73.6 us -> 63.4 us  [body(): pl.pallas_call(functools.partial(step_kernel, xs, zs, n, total), out_shap...]
where the time goes in v4:
time: 69.1 us; the launch traced here: 68.9 us
  Pallas kernels  68.3 us (99%)
    pallas_call x1, Pallas kernels, body(): pl.pallas_call(functools.partial(step_kernel, xs, zs, n, total), out_shap...  63.4 us
    pallas_call x1, Pallas kernels, body(): pl.pallas_call(factor_kernel, out_shape=[jax.ShapeDtypeStruct((3, n), f32...  4.92 us

profile of v4, /device:TPU:1, one launch (start us, length us, event | category | flops | bytes accessed | tf_op | source)
XLA Modules:
  0.0 68.9 jit_solution(645344260193021066)
XLA Ops:
  0.6 63.4 %shard_map.75 = (f32[128,128]{1,0:T(8,128)S(1)}, f32[6,24,128]{2,1,0:T(8,128)S(1)}, f32[3,24]{1,0:T(4,128)S(1)}, f32[3,24]{1,0:T(4,128)S(1)}) custom-call(f32[3,24]{1,0:T(4,128)} %pos_hbm.1, f32[3,24]{1,0:T(4,128)} %vel_hbm.1, f32[1,24]{1,0:T(1,128)} %bitcast.1, f32[6,24,128]{2,1,0:T(8,128)} %tan_hbm.1), custom_call_target="tpu_custom_call" | custom-call | tf_op jit(solution)/shard_map/pallas_call | solution.py:461
  64.0 4.9 %shard_map.76 = (f32[3,24]{1,0:T(4,128)}, f32[3,24]{1,0:T(4,128)}, f32[6,24,128]{2,1,0:T(8,128)}, f32[128,128]{1,0:T(8,128)}) custom-call(f32[128,128]{1,0:T(8,128)S(1)} %get-tuple-element.8.gram_ref, f32[6,24,128]{2,1,0:T(8,128)S(1)} %get-tuple-element.9.mat_ref, f32[3,24]{1,0:T(4,128)S(1)} %get-tuple-element.10.npos_ref, ...), custom_call_target="tpu_custom_call" | custom-call | tf_op jit(solution)/shard_map/pallas_call | solution.py:479

commit v5 on v4

--- a/solution.py
+++ b/solution.py
@@ -18,10 +18,10 @@
 RING = {
     16: (
         {0: (3, -3, 1, -1), 3: (6, 2, 4), -3: (-6, -2, -4), 6: (8, 5, 7), -6: (-5, -7)},
-        ((0, 3, -3, 1, -1), (6, -6, 2, -2, 4, -4), (5, -5, 7, -7, 8)),
+        ((0, 3, -3, 1, -1), (2, -2, 4, -4), (6, -6), (5, -5, 7, -7, 8)),
         3,
     ),
-    4: ({0: (1, -1), 1: (2,)}, ((0, 1), (-1,), (2,)), 1),
+    4: ({0: (1, -1), 1: (2,)}, ((0,), (1,), (-1,), (2,)), 1),
 }
 
 
@@ -63,7 +63,7 @@
     sources = 2 * zs * n
     passes, phases, reach = RING[zs]
     order = [(h, place) for group in phases for h in range(2) for place in group]
-    early = 2 * (len(phases[0]) + len(phases[1])) * n // 128
+    early = 2 * (zs - len(phases[3])) * n // 128
     split = 3 * 128 * early
     width = sources // 128 - early
 
@@ -253,18 +253,19 @@
     joined(phases[0])
     count = 2 * len(phases[0])
     take(count)
-    for place in phases[1]:
+    for place in phases[1] + phases[2]:
         visit(place)
-    joined(phases[1])
-    count += 2 * len(phases[1])
-    take(count)
-    for place in phases[2]:
-        visit(place)
+    for group_of in phases[1:3]:
+        joined(group_of)
+        count += 2 * len(group_of)
+        take(count)
     halves(count)
     if early:
         lax.fori_loop(0, planes // group, early_group, 0)
-    take(count + len(phases[2]))
-    joined(phases[2])
+    for place in phases[3]:
+        visit(place)
+    take(count + len(phases[3]))
+    joined(phases[3])
     take(2 * zs)
 
     halves(2 * zs)
@@ -361,7 +362,9 @@
     for r in line:
         remote(g_mine, g_line.at[zs - r - 1], gs_send.at[1], gs_recv.at[1], line_peer(r)).start()
     line_sums = remote(g_line, g_line, gs_send.at[1], gs_recv.at[1], sibling)
-    pending.append(line_sums.wait_send)
+    for wait in pending:
+        wait()
+    pending = [line_sums.wait_send]
     line_sums.wait_recv()
     for r in range(zs - 1):
         mine = mine + g_line[r]
@@ -400,8 +403,9 @@
         for r in range(8):
             arow, qrow = full(a[b][r:r + 1, :]), full(q[b][r:r + 1, :])
             crow = {e: full(c[b][e][r:r + 1, :]) for e in range(r, 8)}
-            scale = jnp.where(rows == r, lax.rsqrt(crow[r]), scale)
-            inverse = 1.0 / crow[r]
+            root = lax.rsqrt(crow[r])
+            scale = jnp.where(rows == r, root, scale)
+            inverse = root * root
             for i in range(b, count):
                 m = c[i][r] * inverse
                 if i == b:

time: 69.1 us -> 68.8 us (level)
  no operation moved by 1% of the time
where the time goes in v5:
time: 68.8 us; the launch traced here: 68.7 us
  Pallas kernels  68 us (99%)
    pallas_call x1, Pallas kernels, body(): pl.pallas_call(functools.partial(step_kernel, xs, zs, n, total), out_shap...  63 us
    pallas_call x1, Pallas kernels, body(): pl.pallas_call(factor_kernel, out_shape=[jax.ShapeDtypeStruct((3, n), f32...  5.09 us

profile of v5, /device:TPU:1, one launch (start us, length us, event | category | flops | bytes accessed | tf_op | source)
XLA Modules:
  0.0 68.7 jit_solution(7933320595731656035)
XLA Ops:
  0.6 63.0 %shard_map.75 = (f32[128,128]{1,0:T(8,128)S(1)}, f32[6,24,128]{2,1,0:T(8,128)S(1)}, f32[3,24]{1,0:T(4,128)S(1)}, f32[3,24]{1,0:T(4,128)S(1)}) custom-call(f32[3,24]{1,0:T(4,128)} %pos_hbm.1, f32[3,24]{1,0:T(4,128)} %vel_hbm.1, f32[1,24]{1,0:T(1,128)} %bitcast.1, f32[6,24,128]{2,1,0:T(8,128)} %tan_hbm.1), custom_call_target="tpu_custom_call" | custom-call | tf_op jit(solution)/shard_map/pallas_call | solution.py:465
  63.6 5.1 %shard_map.76 = (f32[3,24]{1,0:T(4,128)}, f32[3,24]{1,0:T(4,128)}, f32[6,24,128]{2,1,0:T(8,128)}, f32[128,128]{1,0:T(8,128)}) custom-call(f32[128,128]{1,0:T(8,128)S(1)} %get-tuple-element.8.gram_ref, f32[6,24,128]{2,1,0:T(8,128)S(1)} %get-tuple-element.9.mat_ref, f32[3,24]{1,0:T(4,128)S(1)} %get-tuple-element.10.npos_ref, ...), custom_call_target="tpu_custom_call" | custom-call | tf_op jit(solution)/shard_map/pallas_call | solution.py:483

commit v6 on v5

--- a/solution.py
+++ b/solution.py
@@ -403,9 +403,8 @@
         for r in range(8):
             arow, qrow = full(a[b][r:r + 1, :]), full(q[b][r:r + 1, :])
             crow = {e: full(c[b][e][r:r + 1, :]) for e in range(r, 8)}
-            root = lax.rsqrt(crow[r])
-            scale = jnp.where(rows == r, root, scale)
-            inverse = root * root
+            scale = jnp.where(rows == r, lax.rsqrt(crow[r]), scale)
+            inverse = 1.0 / crow[r]
             for i in range(b, count):
                 m = c[i][r] * inverse
                 if i == b:

time: 68.8 us -> 68.7 us (level)
  no operation moved by 1% of the time
where the time goes in v6:
time: 68.7 us; the launch traced here: 68.5 us
  Pallas kernels  67.9 us (99%)
    pallas_call x1, Pallas kernels, body(): pl.pallas_call(functools.partial(step_kernel, xs, zs, n, total), out_shap...  63 us
    pallas_call x1, Pallas kernels, body(): pl.pallas_call(factor_kernel, out_shape=[jax.ShapeDtypeStruct((3, n), f32...  4.92 us

profile of v6, /device:TPU:1, one launch (start us, length us, event | category | flops | bytes accessed | tf_op | source)
XLA Modules:
  0.0 68.5 jit_solution(12185419302154999284)
XLA Ops:
  0.6 63.0 %shard_map.75 = (f32[128,128]{1,0:T(8,128)S(1)}, f32[6,24,128]{2,1,0:T(8,128)S(1)}, f32[3,24]{1,0:T(4,128)S(1)}, f32[3,24]{1,0:T(4,128)S(1)}) custom-call(f32[3,24]{1,0:T(4,128)} %pos_hbm.1, f32[3,24]{1,0:T(4,128)} %vel_hbm.1, f32[1,24]{1,0:T(1,128)} %bitcast.1, f32[6,24,128]{2,1,0:T(8,128)} %tan_hbm.1), custom_call_target="tpu_custom_call" | custom-call | tf_op jit(solution)/shard_map/pallas_call | solution.py:464
  63.6 4.9 %shard_map.76 = (f32[3,24]{1,0:T(4,128)}, f32[3,24]{1,0:T(4,128)}, f32[6,24,128]{2,1,0:T(8,128)}, f32[128,128]{1,0:T(8,128)}) custom-call(f32[128,128]{1,0:T(8,128)S(1)} %get-tuple-element.8.gram_ref, f32[6,24,128]{2,1,0:T(8,128)S(1)} %get-tuple-element.9.mat_ref, f32[3,24]{1,0:T(4,128)S(1)} %get-tuple-element.10.npos_ref, ...), custom_call_target="tpu_custom_call" | custom-call | tf_op jit(solution)/shard_map/pallas_call | solution.py:482
